TPU v7x, 32 devices: a whole 2x2x4 slice. The times are simulated.
32 devices in a mesh: region: 8 (over z, y), chan: 4 (over x, core).
Axes of the slice: x: 2, y: 2, z: 4, core: 2. Of those that a mesh axis runs over, the one named last changes fastest.
Arguments:
- grid_state: bfloat16 [8192, 1024], P('region', 'chan'), may hold values from -6 to 6
- mesh_state: bfloat16 [2048, 1024], P('region', 'chan'), may hold values from -6 to 6
- enc_send: bfloat16 [1024, 1024], P(None, 'chan'), may hold values from -0.1875 to 0.1875
- enc_out: bfloat16 [1024, 1024], P(None, 'chan'), may hold values from -0.1875 to 0.1875
- proc_send: bfloat16 [1024, 1024], P(None, 'chan'), may hold values from -0.1875 to 0.1875
- proc_out: bfloat16 [1024, 1024], P(None, 'chan'), may hold values from -0.1875 to 0.1875
- dec_send: bfloat16 [1024, 1024], P(None, 'chan'), may hold values from -0.1875 to 0.1875
- dec_out: bfloat16 [1024, 1024], P(None, 'chan'), may hold values from -0.1875 to 0.1875
- g2m_index: int32 [16, 2048], P(None, 'region'), may hold values from 0 to 8191, as said below
- g2m_weight: float32 [16, 2048], P(None, 'region'), may hold values from 0.25 to 4
- g2m_count: int32 [2048], P('region'), may hold values from 1 to 16
- m2m_index: int32 [8, 2048], P(None, 'region'), may hold values from 0 to 2047, as said below
- m2m_weight: float32 [8, 2048], P(None, 'region'), may hold values from 0.25 to 4
- m2m_count: int32 [2048], P('region'), may hold values from 1 to 8
- m2g_index: int32 [4, 8192], P(None, 'region'), may hold values from 0 to 2047, as said below
- m2g_weight: float32 [4, 8192], P(None, 'region'), may hold values from 0.25 to 4
- m2g_count: int32 [8192], P('region'), may hold values from 1 to 4
Outputs:
- grid_next: bfloat16 [8192, 1024], P('region', 'chan')
- mesh_next: bfloat16 [2048, 1024], P('region', 'chan')
Inputs may be any that keep to these rules, and one draw needn't show every extreme that they name: Column i of g2m_index belongs to mesh node i, of region i // 256; each entry names a grid node whose region (index // 1024) differs from it by at most 2. `m2m_index`: column i belongs to mesh node i, of region i // 256; each entry names a mesh node whose region (index // 256) differs from it by at most 2. `m2g_index`: column i belongs to grid node i, of region i // 1024; each entry names a mesh node whose region (index // 256) differs from it by at most 2.
All inputs are finite; a program needn't handle non-finite values.
Results may differ from a plain program's by a relative error of at most 0.017.
Values may be sent and summed in bfloat16 or wider, within the bound.
A program may use at most 64 MiB of HBM per device.

v0:
```python
import jax
import jax.numpy as jnp
from jax import lax
from jax.sharding import PartitionSpec as P

SPAN = 2


def from_behind(shard, axis, by):
    devices = lax.axis_size(axis)
    pairs = [(i, i + by) for i in range(devices) if 0 <= i + by < devices]
    return lax.ppermute(shard, axis, pairs)


def project(values, weight):
    return jnp.dot(
        lax.all_gather(values, "chan", axis=1, tiled=True),
        weight,
        preferred_element_type=jnp.float32,
    )


def neighbourhood(projected):
    fetched = {}
    for offset in [o for o in range(1, SPAN + 1)] + [-o for o in range(1, SPAN + 1)]:
        fetched[offset] = from_behind(projected, "region", offset)
    ordered = (
        [fetched[o] for o in range(SPAN, 0, -1)]
        + [projected]
        + [fetched[-o] for o in range(1, SPAN + 1)]
    )
    return jnp.concatenate(ordered, axis=0)


def messages(projected, receivers, index_block, edge_weight, counts):
    slots = index_block.shape[0]
    fetched = jnp.take(projected, index_block, axis=0).astype(jnp.float32)
    message = jax.nn.silu(fetched + receivers.astype(jnp.float32)[None]) * edge_weight[:, :, None]
    valid = jnp.arange(slots, dtype=jnp.int32)[:, None] < counts[None, :]
    summed = jnp.sum(jnp.where(valid[:, :, None], message, 0.0), axis=0)
    return (summed / counts.astype(jnp.float32)[:, None]).astype(jnp.bfloat16)


def pulled_aggregate(projected, receivers, index_block, edge_weight, counts):
    window = neighbourhood(projected)
    first_row = (lax.axis_index("region") - SPAN) * projected.shape[0]
    local_index = index_block - first_row
    return messages(window, receivers, local_index, edge_weight, counts)


def finish(receivers, aggregate, w_out):
    return (receivers.astype(jnp.float32) + project(aggregate, w_out)).astype(jnp.bfloat16)


def layer(senders, receivers, w_send, w_out, index_block, edge_weight, counts):
    projected = project(senders, w_send).astype(jnp.bfloat16)
    aggregate = pulled_aggregate(projected, receivers, index_block, edge_weight, counts)
    return finish(receivers, aggregate, w_out)


def shards(
    grid_state,
    mesh_state,
    enc_send,
    enc_out,
    proc_send,
    proc_out,
    dec_send,
    dec_out,
    g2m_index,
    g2m_weight,
    g2m_count,
    m2m_index,
    m2m_weight,
    m2m_count,
    m2g_index,
    m2g_weight,
    m2g_count,
):
    mesh_one = layer(grid_state, mesh_state, enc_send, enc_out, g2m_index, g2m_weight, g2m_count)
    mesh_next = layer(mesh_one, mesh_one, proc_send, proc_out, m2m_index, m2m_weight, m2m_count)
    grid_next = layer(mesh_next, grid_state, dec_send, dec_out, m2g_index, m2g_weight, m2g_count)
    return (grid_next, mesh_next)


def solution(mesh):
    placed = (
        P("region", "chan"),
        P("region", "chan"),
        P(None, "chan"),
        P(None, "chan"),
        P(None, "chan"),
        P(None, "chan"),
        P(None, "chan"),
        P(None, "chan"),
        P(None, "region"),
        P(None, "region"),
        P("region"),
        P(None, "region"),
        P(None, "region"),
        P("region"),
        P(None, "region"),
        P(None, "region"),
        P("region"),
    )
    return jax.shard_map(
        shards,
        mesh=mesh,
        in_specs=placed,
        out_specs=(P("region", "chan"), P("region", "chan")),
        check_vma=False,
    )
```

profile of v0, /device:TPU:1, one launch (start us, length us, event | category | flops | bytes accessed | tf_op | source)
XLA Modules:
  0.0 219.1 jit_solution(8710304745878100532)
XLA Ops:
  7.2 0.0 copy-start
  7.2 0.0 all-gather.3.cloned.1.call-start
  7.2 0.7 all-gather.3.cloned.1.call-update
  7.9 0.0 all-gather.5.cloned.1.call-start
  8.0 0.7 fusion.3
  8.7 0.6 broadcast_clamp_fusion
  9.3 0.7 fusion.4
  10.1 0.0 copy-start.10
  10.1 0.0 copy-start.18
  10.1 0.0 copy-start.4
  10.1 24.8 %all-gather.3.cloned.1.call-done = bf16[1024,1024]{1,0:T(8,128)(2,1)} async-done(((bf16[1024,256]{1,0:T(8,128)(2,1)}), bf16[1024,1024]{1,0:T(8,128)(2,1)}) %all-gather.3.cloned.1.call-update) | async-done | bytes 2097168 | tf_op jit(solution)/shard_map/all_gather | solution.py:17
  34.9 2.3 %convolution_convert_fusion = bf16[1024,256]{1,0:T(8,128)(2,1)S(1)} fusion(bf16[1024,1024]{1,0:T(8,128)(2,1)} %all-gather.3.cloned.1.call-done, bf16[1024,256]{1,0:T(8,128)(2,1)S(1)} %copy-done), kind=kOutput, calls=%fused_computation.7 | convolution fusion | flops 537133056 | bytes 3145728 | tf_op jit(solution)/shard_map/dot_general | solution.py:16
  37.2 3.1 %collective-permute-start = (bf16[1024,256]{1,0:T(8,128)(2,1)S(1)}, bf16[1024,256]{1,0:T(8,128)(2,1)S(1)}, u32[]{:S(2)}, u32[]{:S(2)}) collective-permute-start(bf16[1024,256]{1,0:T(8,128)(2,1)S(1)} %convolution_convert_fusion), channel_id=1, source_target_pairs={{0,8},{4,12},{8,16},{12,20},{16,24},{20,28},{1,9},{5,13},{9,17},{1... | collective-permute-start | bytes 1572872 | tf_op jit(solution)/shard_map/ppermute | solution.py:12
  40.4 3.1 %collective-permute-start.1 = (bf16[1024,256]{1,0:T(8,128)(2,1)S(1)}, bf16[1024,256]{1,0:T(8,128)(2,1)S(1)}, u32[]{:S(2)}, u32[]{:S(2)}) collective-permute-start(bf16[1024,256]{1,0:T(8,128)(2,1)S(1)} %convolution_convert_fusion), channel_id=1, source_target_pairs={{0,4},{4,8},{8,12},{12,16},{16,20},{20,24},{24,28},{1,5},{5,9},{9,... | collective-permute-start | bytes 1572872 | tf_op jit(solution)/shard_map/ppermute | solution.py:12
  43.6 0.6 iota_compare_fusion
  44.2 1.3 collective-permute-start.2
  45.5 1.3 collective-permute-start.3
  46.8 0.6 broadcast_clamp_fusion.1
  47.4 0.6 convert_element_type.61
  48.0 3.4 %collective-permute-done = bf16[1024,256]{1,0:T(8,128)(2,1)S(1)} collective-permute-done((bf16[1024,256]{1,0:T(8,128)(2,1)S(1)}, bf16[1024,256]{1,0:T(8,128)(2,1)S(1)}, u32[]{:S(2)}, u32[]{:S(2)}) %collective-permute-start) | collective-permute-done | bytes 524320 | tf_op jit(solution)/shard_map/ppermute | solution.py:12
  51.5 14.1 %collective-permute-done.1 = bf16[1024,256]{1,0:T(8,128)(2,1)S(1)} collective-permute-done((bf16[1024,256]{1,0:T(8,128)(2,1)S(1)}, bf16[1024,256]{1,0:T(8,128)(2,1)S(1)}, u32[]{:S(2)}, u32[]{:S(2)}) %collective-permute-start.1) | collective-permute-done | bytes 524320 | tf_op jit(solution)/shard_map/ppermute | solution.py:12
  65.6 5.2 %collective-permute-done.3 = bf16[1024,256]{1,0:T(8,128)(2,1)S(1)} collective-permute-done((bf16[1024,256]{1,0:T(8,128)(2,1)S(1)}, bf16[1024,256]{1,0:T(8,128)(2,1)S(1)}, u32[]{:S(2)}, u32[]{:S(2)}) %collective-permute-start.3) | collective-permute-done | bytes 524320 | tf_op jit(solution)/shard_map/ppermute | solution.py:12
  70.9 18.3 %gather_fusion = bf16[4096,256]{1,0:T(8,128)(2,1)} fusion(bf16[5120,256]{1,0:T(8,128)(2,1)S(1)} %constant_dynamic-update-slice_fusion, s32[4096]{0:T(1024)} %broadcast_clamp_fusion), kind=kCustom, calls=%fused_computation | custom fusion | bytes 4210688 | tf_op jit(solution)/shard_map/jit(_take)/gather | solution.py:37
  89.2 5.6 %select_reduce_fusion.1 = f32[256,256]{1,0:T(8,128)S(1)} fusion(f32[16,256]{1,0:T(8,128)} %param.26, f32[256,256]{1,0:T(8,128)S(1)} %convert_element_type.58, bf16[16,256,256]{2,1,0:T(8,128)(2,1)} %bitcast.25, pred[16,256]{1,0:T(8,128)(4,1)} %get-tuple-element.5, pred[16,256]{1,0:T(8,128)(4,1)} %get-tuple-element.4), kind=kLoop, calls=%fused_computation.4 | loop fusion | flops 10420224 | bytes 2646016 | tf_op jit(solution)/shard_map/reduce_sum | solution.py:40
  94.8 0.0 copy-start.12
  94.8 0.0 copy-start.19
  94.8 0.1 divide_convert_fusion.2
  94.9 0.0 copy-start.13
  95.0 8.0 %all_gather.19 = bf16[256,1024]{1,0:T(8,128)(2,1)S(1)} all-gather(bf16[256,256]{1,0:T(8,128)(2,1)S(1)} %divide_convert_fusion.2), channel_id=1, replica_groups=mesh['region'=8,'chan'=4] {'chan'}, dimensions={1}, use_global_device_ids=true | all-gather | bytes 655360 | tf_op jit(solution)/shard_map/all_gather | solution.py:17
  103.0 0.3 fusion.6
  103.3 7.3 %all_gather.20 = bf16[256,1024]{1,0:T(8,128)(2,1)S(1)} all-gather(bf16[256,256]{1,0:T(8,128)(2,1)S(1)} %get-tuple-element.3), channel_id=1, replica_groups=mesh['region'=8,'chan'=4] {'chan'}, dimensions={1}, use_global_device_ids=true | all-gather | bytes 655360 | tf_op jit(solution)/shard_map/all_gather | solution.py:17
  110.6 0.3 convolution_convert_fusion.2
  110.9 3.1 %collective-permute-start.4 = (bf16[256,256]{1,0:T(8,128)(2,1)S(1)}, bf16[256,256]{1,0:T(8,128)(2,1)S(1)}, u32[]{:S(2)}, u32[]{:S(2)}) collective-permute-start(bf16[256,256]{1,0:T(8,128)(2,1)S(1)} %convolution_convert_fusion.2), channel_id=1, source_target_pairs={{0,8},{4,12},{8,16},{12,20},{16,24},{20,28},{1,9},{5,13},{9,17},{1... | collective-permute-start | bytes 393224 | tf_op jit(solution)/shard_map/ppermute | solution.py:12
  114.0 1.3 collective-permute-start.5
  115.4 1.3 collective-permute-start.6
  116.7 1.3 collective-permute-start.7
  118.0 0.0 collective-permute-done.5
  118.1 4.5 %collective-permute-done.6 = bf16[256,256]{1,0:T(8,128)(2,1)S(1)} collective-permute-done((bf16[256,256]{1,0:T(8,128)(2,1)S(1)}, bf16[256,256]{1,0:T(8,128)(2,1)S(1)}, u32[]{:S(2)}, u32[]{:S(2)}) %collective-permute-start.6) | collective-permute-done | bytes 131104 | tf_op jit(solution)/shard_map/ppermute | solution.py:12
  122.5 3.9 %collective-permute-done.7 = bf16[256,256]{1,0:T(8,128)(2,1)S(1)} collective-permute-done((bf16[256,256]{1,0:T(8,128)(2,1)S(1)}, bf16[256,256]{1,0:T(8,128)(2,1)S(1)}, u32[]{:S(2)}, u32[]{:S(2)}) %collective-permute-start.7) | collective-permute-done | bytes 131104 | tf_op jit(solution)/shard_map/ppermute | solution.py:12
  126.5 0.0 copy-start.16
  126.5 7.5 %gather_fusion.1 = bf16[2048,256]{1,0:T(8,128)(2,1)S(1)} fusion(bf16[1280,256]{1,0:T(8,128)(2,1)S(1)} %constant_dynamic-update-slice_fusion.5, s32[2048]{0:T(1024)S(1)} %copy-done.13), kind=kCustom, calls=%fused_computation.1 | custom fusion | bytes 2105344 | tf_op jit(solution)/shard_map/jit(_take)/gather | solution.py:37
  134.0 0.0 copy-start.7
  134.0 0.0 copy-start.8
  134.0 0.0 copy-start.9
  134.1 1.2 select_reduce_fusion.2
  135.3 0.1 divide_convert_fusion.1
  135.4 8.0 %all_gather.21 = bf16[256,1024]{1,0:T(8,128)(2,1)S(1)} all-gather(bf16[256,256]{1,0:T(8,128)(2,1)S(1)} %divide_convert_fusion.1), channel_id=1, replica_groups=mesh['region'=8,'chan'=4] {'chan'}, dimensions={1}, use_global_device_ids=true | all-gather | bytes 655360 | tf_op jit(solution)/shard_map/all_gather | solution.py:17
  143.5 0.3 fusion.2
  143.8 0.0 copy-start.5
  143.8 7.3 %all_gather.22 = bf16[256,1024]{1,0:T(8,128)(2,1)S(1)} all-gather(bf16[256,256]{1,0:T(8,128)(2,1)S(1)} %fusion.2), channel_id=1, replica_groups=mesh['region'=8,'chan'=4] {'chan'}, dimensions={1}, use_global_device_ids=true | all-gather | bytes 655360 | tf_op jit(solution)/shard_map/all_gather | solution.py:17
  151.1 0.3 convolution_convert_fusion.1
  151.4 2.5 %collective-permute-start.8 = (bf16[256,256]{1,0:T(8,128)(2,1)S(1)}, bf16[256,256]{1,0:T(8,128)(2,1)S(1)}, u32[]{:S(2)}, u32[]{:S(2)}) collective-permute-start(bf16[256,256]{1,0:T(8,128)(2,1)S(1)} %convolution_convert_fusion.1), channel_id=1, source_target_pairs={{0,8},{4,12},{8,16},{12,20},{16,24},{20,28},{1,9},{5,13},{9,17},{1... | collective-permute-start | bytes 393224 | tf_op jit(solution)/shard_map/ppermute | solution.py:12
  153.9 1.3 collective-permute-start.9
  155.3 1.1 convert_element_type.57
  156.4 1.3 collective-permute-start.10
  157.6 1.3 collective-permute-start.11
  159.0 4.3 %collective-permute-done.10 = bf16[256,256]{1,0:T(8,128)(2,1)S(1)} collective-permute-done((bf16[256,256]{1,0:T(8,128)(2,1)S(1)}, bf16[256,256]{1,0:T(8,128)(2,1)S(1)}, u32[]{:S(2)}, u32[]{:S(2)}) %collective-permute-start.10) | collective-permute-done | bytes 131104 | tf_op jit(solution)/shard_map/ppermute | solution.py:12
  163.3 3.9 %collective-permute-done.11 = bf16[256,256]{1,0:T(8,128)(2,1)S(1)} collective-permute-done((bf16[256,256]{1,0:T(8,128)(2,1)S(1)}, bf16[256,256]{1,0:T(8,128)(2,1)S(1)}, u32[]{:S(2)}, u32[]{:S(2)}) %collective-permute-start.11) | collective-permute-done | bytes 131104 | tf_op jit(solution)/shard_map/ppermute | solution.py:12
  167.2 14.6 %gather_fusion.2 = bf16[4096,256]{1,0:T(8,128)(2,1)S(1)} fusion(bf16[1280,256]{1,0:T(8,128)(2,1)S(1)} %constant_dynamic-update-slice_fusion.10, s32[4096]{0:T(1024)S(1)} %bitcast_clamp_fusion), kind=kCustom, calls=%fused_computation.2 | custom fusion | bytes 4210688 | tf_op jit(solution)/shard_map/jit(_take)/gather | solution.py:37
  181.9 5.3 %select_reduce_fusion = f32[1024,256]{1,0:T(8,128)S(1)} fusion(f32[4,1024]{1,0:T(4,128)S(1)} %copy-done.14, f32[1024,256]{1,0:T(8,128)} %convert_element_type.57, bf16[4,1024,256]{2,1,0:T(8,128)(2,1)S(1)} %bitcast.26, pred[4,1024]{1,0:T(4,128)(4,1)S(1)} %get-tuple-element.9, pred[4,1024]{1,0:T(4,128)(4,1)S(1)} %get-tuple-element.8), kind=kLoop, calls=%fused_computation.3 | loop fusion | flops 10223616 | bytes 4218880 | tf_op jit(solution)/shard_map/reduce_sum | solution.py:40
  187.1 1.0 divide_convert_fusion
  188.1 0.0 all-gather.5.cloned.1.call-update
  188.2 20.9 %all-gather.5.cloned.1.call-done = bf16[1024,1024]{1,0:T(8,128)(2,1)} async-done(((bf16[1024,256]{1,0:T(8,128)(2,1)}), bf16[1024,1024]{1,0:T(8,128)(2,1)}) %all-gather.5.cloned.1.call-update) | async-done | bytes 2097168 | tf_op jit(solution)/shard_map/all_gather | solution.py:17
  209.1 3.2 %fusion = bf16[1024,256]{1,0:T(8,128)(2,1)} fusion(bf16[1024,1024]{1,0:T(8,128)(2,1)} %all-gather.5.cloned.1.call-done, bf16[1024,256]{1,0:T(8,128)(2,1)} %param.24, bf16[1024,256]{1,0:T(8,128)(2,1)S(1)} %copy-done.2), kind=kOutput, calls=%fused_computation.8 | convolution fusion | flops 537657344 | bytes 3670016 | tf_op jit(solution)/shard_map/dot_general | solution.py:16
  (56 shorter events, 0.4 us)
Async XLA Ops:
  7.2 27.8 %copy-start = (bf16[1024,256]{1,0:T(8,128)(2,1)S(1)}, bf16[1024,256]{1,0:T(8,128)(2,1)}, u32[]{:S(2)}) copy-start(bf16[1024,256]{1,0:T(8,128)(2,1)} %param.19) | copy-start | bytes 1572868
  7.2 27.8 %all-gather.3.cloned.1.call-start = ((), (), s32[]{:S(2)}) async-start(), calls=%async_computation | async-start | bytes 2621440 | tf_op jit(solution)/shard_map/all_gather | solution.py:17
  7.9 201.2 %all-gather.5.cloned.1.call-start = ((), (), s32[]{:S(2)}) async-start(), calls=%async_computation.1 | async-start | bytes 2621440 | tf_op jit(solution)/shard_map/all_gather | solution.py:17
  10.0 30.3 %copy-start.11 = (s32[8,256]{1,0:T(8,128)S(1)}, s32[8,256]{1,0:T(8,128)}, u32[]{:S(2)}) copy-start(s32[8,256]{1,0:T(8,128)} %param.28) | copy-start | bytes 24580
  10.1 33.5 %copy-start.10 = (s32[16,256]{1,0:T(8,128)S(1)}, s32[16,256]{1,0:T(8,128)}, u32[]{:S(2)}) copy-start(s32[16,256]{1,0:T(8,128)} %param.25) | copy-start | bytes 49156
  10.1 33.5 %copy-start.18 = (s32[256]{0:T(256)S(1)}, s32[256]{0:T(256)}, u32[]{:S(2)}) copy-start(s32[256]{0:T(256)} %param.27) | copy-start | bytes 3076
  10.1 37.9 %copy-start.4 = (bf16[256,256]{1,0:T(8,128)(2,1)S(1)}, bf16[256,256]{1,0:T(8,128)(2,1)}, u32[]{:S(2)}) copy-start(bf16[256,256]{1,0:T(8,128)(2,1)} %param.18) | copy-start | bytes 393220
  37.2 14.2 %collective-permute-start = (bf16[1024,256]{1,0:T(8,128)(2,1)S(1)}, bf16[1024,256]{1,0:T(8,128)(2,1)S(1)}, u32[]{:S(2)}, u32[]{:S(2)}) collective-permute-start(bf16[1024,256]{1,0:T(8,128)(2,1)S(1)} %convolution_convert_fusion), channel_id=1, source_target_pairs={{0,8},{4,12},{8,16},{12,20},{16,24},{20,28},{1,9},{5,13},{9,17},{1... | collective-permute-start | bytes 1572872 | tf_op jit(solution)/shard_map/ppermute | solution.py:12
  40.4 25.1 %collective-permute-start.1 = (bf16[1024,256]{1,0:T(8,128)(2,1)S(1)}, bf16[1024,256]{1,0:T(8,128)(2,1)S(1)}, u32[]{:S(2)}, u32[]{:S(2)}) collective-permute-start(bf16[1024,256]{1,0:T(8,128)(2,1)S(1)} %convolution_convert_fusion), channel_id=1, source_target_pairs={{0,4},{4,8},{8,12},{12,16},{16,20},{20,24},{24,28},{1,5},{5,9},{9,... | collective-permute-start | bytes 1572872 | tf_op jit(solution)/shard_map/ppermute | solution.py:12
  44.2 21.4 %collective-permute-start.2 = (bf16[1024,256]{1,0:T(8,128)(2,1)S(1)}, bf16[1024,256]{1,0:T(8,128)(2,1)S(1)}, u32[]{:S(2)}, u32[]{:S(2)}) collective-permute-start(bf16[1024,256]{1,0:T(8,128)(2,1)S(1)} %convolution_convert_fusion), channel_id=1, source_target_pairs={{4,0},{8,4},{12,8},{16,12},{20,16},{24,20},{28,24},{5,1},{9,5},{13... | collective-permute-start | bytes 1572872 | tf_op jit(solution)/shard_map/ppermute | solution.py:12
  45.5 25.4 %collective-permute-start.3 = (bf16[1024,256]{1,0:T(8,128)(2,1)S(1)}, bf16[1024,256]{1,0:T(8,128)(2,1)S(1)}, u32[]{:S(2)}, u32[]{:S(2)}) collective-permute-start(bf16[1024,256]{1,0:T(8,128)(2,1)S(1)} %convolution_convert_fusion), channel_id=1, source_target_pairs={{8,0},{12,4},{16,8},{20,12},{24,16},{28,20},{9,1},{13,5},{17,9},{2... | collective-permute-start | bytes 1572872 | tf_op jit(solution)/shard_map/ppermute | solution.py:12
  89.2 5.6 %copy-start.17 = (f32[256]{0:T(256)S(1)}, f32[256]{0:T(256)}, u32[]{:S(2)}) copy-start(f32[256]{0:T(256)} %convert_element_type.61) | copy-start | bytes 3076
  89.2 13.8 %copy-start.3 = (bf16[1024,256]{1,0:T(8,128)(2,1)S(1)}, bf16[1024,256]{1,0:T(8,128)(2,1)}, u32[]{:S(2)}) copy-start(bf16[1024,256]{1,0:T(8,128)(2,1)} %param.20) | copy-start | bytes 1572868
  89.2 21.4 %copy-start.6 = (bf16[1024,256]{1,0:T(8,128)(2,1)S(1)}, bf16[1024,256]{1,0:T(8,128)(2,1)}, u32[]{:S(2)}) copy-start(bf16[1024,256]{1,0:T(8,128)(2,1)} %param.21) | copy-start | bytes 1572868
  94.8 20.5 %copy-start.12 = (s32[8,256]{1,0:T(8,128)S(1)}, s32[8,256]{1,0:T(8,128)}, u32[]{:S(2)}) copy-start(s32[8,256]{1,0:T(8,128)} %param.28) | copy-start | bytes 24580
  94.8 20.5 %copy-start.19 = (s32[256]{0:T(256)S(1)}, s32[256]{0:T(256)}, u32[]{:S(2)}) copy-start(s32[256]{0:T(256)} %param.30) | copy-start | bytes 3076
  94.9 31.5 %copy-start.13 = (s32[2048]{0:T(1024)S(1)}, s32[2048]{0:T(1024)}, u32[]{:S(2)}) copy-start(s32[2048]{0:T(1024)} %broadcast_clamp_fusion.1) | copy-start | bytes 24580
  110.9 7.1 %collective-permute-start.4 = (bf16[256,256]{1,0:T(8,128)(2,1)S(1)}, bf16[256,256]{1,0:T(8,128)(2,1)S(1)}, u32[]{:S(2)}, u32[]{:S(2)}) collective-permute-start(bf16[256,256]{1,0:T(8,128)(2,1)S(1)} %convolution_convert_fusion.2), channel_id=1, source_target_pairs={{0,8},{4,12},{8,16},{12,20},{16,24},{20,28},{1,9},{5,13},{9,17},{1... | collective-permute-start | bytes 393224 | tf_op jit(solution)/shard_map/ppermute | solution.py:12
  114.0 4.0 %collective-permute-start.5 = (bf16[256,256]{1,0:T(8,128)(2,1)S(1)}, bf16[256,256]{1,0:T(8,128)(2,1)S(1)}, u32[]{:S(2)}, u32[]{:S(2)}) collective-permute-start(bf16[256,256]{1,0:T(8,128)(2,1)S(1)} %convolution_convert_fusion.2), channel_id=1, source_target_pairs={{0,4},{4,8},{8,12},{12,16},{16,20},{20,24},{24,28},{1,5},{5,9},{9,... | collective-permute-start | bytes 393224 | tf_op jit(solution)/shard_map/ppermute | solution.py:12
  115.4 7.2 %collective-permute-start.6 = (bf16[256,256]{1,0:T(8,128)(2,1)S(1)}, bf16[256,256]{1,0:T(8,128)(2,1)S(1)}, u32[]{:S(2)}, u32[]{:S(2)}) collective-permute-start(bf16[256,256]{1,0:T(8,128)(2,1)S(1)} %convolution_convert_fusion.2), channel_id=1, source_target_pairs={{4,0},{8,4},{12,8},{16,12},{20,16},{24,20},{28,24},{5,1},{9,5},{13... | collective-permute-start | bytes 393224 | tf_op jit(solution)/shard_map/ppermute | solution.py:12
  116.7 9.8 %collective-permute-start.7 = (bf16[256,256]{1,0:T(8,128)(2,1)S(1)}, bf16[256,256]{1,0:T(8,128)(2,1)S(1)}, u32[]{:S(2)}, u32[]{:S(2)}) collective-permute-start(bf16[256,256]{1,0:T(8,128)(2,1)S(1)} %convolution_convert_fusion.2), channel_id=1, source_target_pairs={{8,0},{12,4},{16,8},{20,12},{24,16},{28,20},{9,1},{13,5},{17,9},{2... | collective-permute-start | bytes 393224 | tf_op jit(solution)/shard_map/ppermute | solution.py:12
  126.5 7.5 %copy-start.16 = (f32[8,256]{1,0:T(8,128)S(1)}, f32[8,256]{1,0:T(8,128)}, u32[]{:S(2)}) copy-start(f32[8,256]{1,0:T(8,128)} %param.29) | copy-start | bytes 24580
  134.0 9.5 %copy-start.7 = (bf16[1024,256]{1,0:T(8,128)(2,1)S(1)}, bf16[1024,256]{1,0:T(8,128)(2,1)}, u32[]{:S(2)}) copy-start(bf16[1024,256]{1,0:T(8,128)(2,1)} %param.22) | copy-start | bytes 1572868
  134.0 17.1 %copy-start.8 = (bf16[1024,256]{1,0:T(8,128)(2,1)S(1)}, bf16[1024,256]{1,0:T(8,128)(2,1)}, u32[]{:S(2)}) copy-start(bf16[1024,256]{1,0:T(8,128)(2,1)} %param.23) | copy-start | bytes 1572868
  134.0 21.2 %copy-start.9 = (s32[4,1024]{1,0:T(4,128)S(1)}, s32[4,1024]{1,0:T(4,128)}, u32[]{:S(2)}) copy-start(s32[4,1024]{1,0:T(4,128)} %param.31) | copy-start | bytes 49156
  134.1 21.2 %copy-start.15 = (s32[1024]{0:T(1024)S(1)}, s32[1024]{0:T(1024)}, u32[]{:S(2)}) copy-start(s32[1024]{0:T(1024)} %param.33) | copy-start | bytes 12292
  134.1 21.2 %copy-start.1 = (bf16[1024,256]{1,0:T(8,128)(2,1)S(1)}, bf16[1024,256]{1,0:T(8,128)(2,1)}, u32[]{:S(2)}) copy-start(bf16[1024,256]{1,0:T(8,128)(2,1)} %param.17) | copy-start | bytes 1572868
  143.8 38.0 %copy-start.5 = (bf16[256,256]{1,0:T(8,128)(2,1)}, bf16[256,256]{1,0:T(8,128)(2,1)S(1)}, u32[]{:S(2)}) copy-start(bf16[256,256]{1,0:T(8,128)(2,1)S(1)} %fusion.2) | copy-start | bytes 393220
  151.4 7.6 %collective-permute-start.8 = (bf16[256,256]{1,0:T(8,128)(2,1)S(1)}, bf16[256,256]{1,0:T(8,128)(2,1)S(1)}, u32[]{:S(2)}, u32[]{:S(2)}) collective-permute-start(bf16[256,256]{1,0:T(8,128)(2,1)S(1)} %convolution_convert_fusion.1), channel_id=1, source_target_pairs={{0,8},{4,12},{8,16},{12,20},{16,24},{20,28},{1,9},{5,13},{9,17},{1... | collective-permute-start | bytes 393224 | tf_op jit(solution)/shard_map/ppermute | solution.py:12
  153.9 5.0 %collective-permute-start.9 = (bf16[256,256]{1,0:T(8,128)(2,1)S(1)}, bf16[256,256]{1,0:T(8,128)(2,1)S(1)}, u32[]{:S(2)}, u32[]{:S(2)}) collective-permute-start(bf16[256,256]{1,0:T(8,128)(2,1)S(1)} %convolution_convert_fusion.1), channel_id=1, source_target_pairs={{0,4},{4,8},{8,12},{12,16},{16,20},{20,24},{24,28},{1,5},{5,9},{9,... | collective-permute-start | bytes 393224 | tf_op jit(solution)/shard_map/ppermute | solution.py:12
  156.4 6.9 %collective-permute-start.10 = (bf16[256,256]{1,0:T(8,128)(2,1)S(1)}, bf16[256,256]{1,0:T(8,128)(2,1)S(1)}, u32[]{:S(2)}, u32[]{:S(2)}) collective-permute-start(bf16[256,256]{1,0:T(8,128)(2,1)S(1)} %convolution_convert_fusion.1), channel_id=1, source_target_pairs={{4,0},{8,4},{12,8},{16,12},{20,16},{24,20},{28,24},{5,1},{9,5},{13... | collective-permute-start | bytes 393224 | tf_op jit(solution)/shard_map/ppermute | solution.py:12
  157.6 9.5 %collective-permute-start.11 = (bf16[256,256]{1,0:T(8,128)(2,1)S(1)}, bf16[256,256]{1,0:T(8,128)(2,1)S(1)}, u32[]{:S(2)}, u32[]{:S(2)}) collective-permute-start(bf16[256,256]{1,0:T(8,128)(2,1)S(1)} %convolution_convert_fusion.1), channel_id=1, source_target_pairs={{8,0},{12,4},{16,8},{20,12},{24,16},{28,20},{9,1},{13,5},{17,9},{2... | collective-permute-start | bytes 393224 | tf_op jit(solution)/shard_map/ppermute | solution.py:12
  167.2 14.6 %copy-start.14 = (f32[4,1024]{1,0:T(4,128)S(1)}, f32[4,1024]{1,0:T(4,128)}, u32[]{:S(2)}) copy-start(f32[4,1024]{1,0:T(4,128)} %param.32) | copy-start | bytes 49156
  181.8 27.3 %copy-start.2 = (bf16[1024,256]{1,0:T(8,128)(2,1)S(1)}, bf16[1024,256]{1,0:T(8,128)(2,1)}, u32[]{:S(2)}) copy-start(bf16[1024,256]{1,0:T(8,128)(2,1)} %param.17) | copy-start | bytes 1572868
Sparse Core Ops, SparseCore 0:
  9.6 25.3 all-gather.2
  188.3 20.7 all-gather.4
where the time goes:
time: 220 us; the launch traced here: 219 us
  waiting for transfers between devices  85.8 us (39%)
  local copies, waits for them, and re-layouts  40.8 us (19%)
  blocking collectives  30.6 us (14%)
  starting transfers between devices  22.3 us (10%)
  other arithmetic  18.3 us (8%)
  between operations  14.6 us (7%)
  matrix products  6.67 us (3%)
    all_gather x2, waiting for transfers between devices, project(): lax.all_gather(values, 'chan', axis=1, tiled=True)  45.8 us
    gather x3, local copies, waits for them, and re-layouts, messages(): fetched = jnp.take(projected, index_block, axis=0).astype(jnp.float32)  40.4 us
    ppermute x12, waiting for transfers between devices, from_behind(): return lax.ppermute(shard, axis, pairs)  39.3 us
    all_gather x4, blocking collectives, project(): lax.all_gather(values, 'chan', axis=1, tiled=True)  30.6 us
    ppermute x12, starting transfers between devices, from_behind(): return lax.ppermute(shard, axis, pairs)  22.3 us
    reduce_sum x3, other arithmetic, messages(): summed = jnp.sum(jnp.where(valid[:, :, None], message, 0.0), axis=0)  12.1 us
    dot_general x6, matrix products, project(): jnp.dot(lax.all_gather(values, 'chan', axis=1, tiled=True), weight, prefe...  6.67 us
  transfers between devices with their start and end apart: 14, of which 9 were waited for; matrix products, arithmetic and copies ran while one was open for 2% of the time, Pallas kernels for 0%

commit v1 on v0

v1 whole, which is shorter than its diff:
```python
import functools

import jax
import jax.numpy as jnp
from jax import lax
from jax.experimental import pallas as pl
from jax.experimental.pallas import tpu as pltpu
from jax.sharding import PartitionSpec as P

SPAN = 2
WIN = 2 * SPAN + 1
OFFSETS = (1, -1, 2, -2)
CH = 4
BF = jnp.bfloat16
F32 = jnp.float32


def kernel(
    n_region,
    grid_state,
    mesh_state,
    enc_send,
    enc_out,
    proc_send,
    proc_out,
    dec_send,
    dec_out,
    ei_ref,
    ew_ref,
    ec_ref,
    pi_ref,
    pw_ref,
    pc_ref,
    di_ref,
    dw_ref,
    dc_ref,
    grid_next,
    mesh_next,
    gbuf,
    msbuf,
    eobuf,
    pobuf,
    etab,
    ptab,
    dtab,
    epos,
    ewt,
    ppos,
    pwt,
    dpos,
    dwt,
    gath,
    agg1,
    agg2,
    agg3,
    m1,
    mn,
    gs_s,
    gs_r,
    ms_s,
    ms_r,
    eo_s,
    eo_r,
    po_s,
    po_r,
    a1_s,
    a1_r,
    a2_s,
    a2_r,
    a3_s,
    a3_r,
    et_s,
    et_r,
    pt_s,
    pt_r,
    dt_s,
    dt_r,
):
    r = lax.axis_index("region")
    c = lax.axis_index("chan")
    c1 = c + 1 - 2 * (c % 2)
    c2 = (c + 2) % 4
    c3 = c2 + 1 - 2 * (c2 % 2)
    rel = (c, c1, c2, c3)
    width = grid_state.shape[1]
    g_rows = grid_state.shape[0]
    m_rows = mesh_state.shape[0]
    cr = g_rows // CH

    def inside(o):
        return jnp.logical_and(r + o >= 0, r + o < n_region)

    barrier = pltpu.get_barrier_semaphore()
    for p in (c1, c2, c3):
        pl.semaphore_signal(barrier, inc=1, device_id=(r, p), device_id_type=pl.DeviceIdType.MESH)
    count = jnp.int32(3)
    for o in OFFSETS:
        ok = inside(o)

        @pl.when(ok)
        def _(o=o):
            pl.semaphore_signal(barrier, inc=1, device_id=(r + o, c), device_id_type=pl.DeviceIdType.MESH)

        count = count + jnp.where(ok, 1, 0)
    pl.semaphore_wait(barrier, count)

    def rcopy(src, dst, ssem, rsem, dev):
        return pltpu.make_async_remote_copy(
            src_ref=src, dst_ref=dst, send_sem=ssem, recv_sem=rsem,
            device_id=dev, device_id_type=pl.DeviceIdType.MESH,
        )

    pending = []

    class Gather:
        def __init__(self, own, slot, ssem, rsem):
            self.to_core = rcopy(own, slot(0), ssem(0), rsem(0), (r, c1))
            self.to_x = rcopy(own, slot(1), ssem(1), rsem(1), (r, c2))
            self.onward = rcopy(slot(1), slot(2), ssem(2), rsem(2), (r, c1))

        def start(self):
            self.to_x.start()
            self.to_core.start()
            pending.append(self)

        def forward(self):
            self.to_x.wait_recv()
            self.onward.start()

        def finish(self):
            self.to_core.wait_recv()
            self.onward.wait_recv()

        def drain(self):
            self.to_core.wait_send()
            self.to_x.wait_send()
            self.onward.wait_send()

    def exchange(tab, ssem, rsem, d):
        return rcopy(tab(0), tab(-d), ssem(d), rsem(-d), ((r + d + n_region) % n_region, c))

    def exchange_start(tab, ssem, rsem):
        for d in OFFSETS:
            @pl.when(inside(d))
            def _(d=d):
                exchange(tab, ssem, rsem, d).start()

    def exchange_recv(tab, ssem, rsem):
        for o in OFFSETS:
            @pl.when(inside(o))
            def _(o=o):
                exchange(tab, ssem, rsem, -o).wait_recv()

    def exchange_drain(tab, ssem, rsem):
        for d in OFFSETS:
            @pl.when(inside(d))
            def _(d=d):
                exchange(tab, ssem, rsem, d).wait_send()

    grid_g = []
    for q in range(CH):
        rows = pl.ds(q * cr, cr)
        g = Gather(
            grid_state.at[rows, :],
            lambda s, q=q: gbuf.at[s, q],
            lambda s, q=q: gs_s.at[s, q],
            lambda s, q=q: gs_r.at[s, q],
        )
        g.start()
        grid_g.append(g)

    def whole(own, buf, ssem, rsem):
        return Gather(own, lambda s: buf.at[s], lambda s: ssem.at[s], lambda s: rsem.at[s])

    ms_g = whole(mesh_state, msbuf, ms_s, ms_r)
    ms_g.start()

    for o in OFFSETS:
        @pl.when(jnp.logical_not(inside(o)))
        def _(o=o):
            for q in range(CH):
                etab[q, o + SPAN] = jnp.zeros((cr, width), BF)
            ptab[o + SPAN] = jnp.zeros((m_rows, width), BF)
            dtab[o + SPAN] = jnp.zeros((m_rows, width), BF)

    def edges(idx_ref, w_ref, cnt_ref, rows_per_region, pos_ref, wt_ref):
        slots, recv = idx_ref.shape
        first = (r - SPAN) * rows_per_region
        tile = m_rows
        for t in range(recv // tile):
            cols = pl.ds(t * tile, tile)
            cnt = cnt_ref[:, cols]
            k = lax.broadcasted_iota(jnp.int32, (slots, tile), 0)
            w = jnp.where(k < cnt, w_ref[:, cols], 0.0) / cnt.astype(F32)
            p = (idx_ref[:, cols] - first).astype(F32)
            pad = jnp.zeros((128 - 2 * slots, tile), F32)
            both = jnp.concatenate([w, p, pad], axis=0).T
            for s in range(slots):
                at = pl.ds((t * slots + s) * tile, tile)
                wt_ref[at, :] = jnp.broadcast_to(both[:, s : s + 1], (tile, 128))
                pos_ref[at, :] = jnp.broadcast_to(
                    both[:, slots + s : slots + s + 1].astype(jnp.int32), (tile, 128)
                ).astype(jnp.int16)

    edges(ei_ref, ew_ref, ec_ref, g_rows, epos, ewt)
    edges(pi_ref, pw_ref, pc_ref, m_rows, ppos, pwt)
    edges(di_ref, dw_ref, dc_ref, m_rows, dpos, dwt)

    def wrows(w_ref, j):
        return w_ref[pl.ds(pl.multiple_of(rel[j] * width, width), width), :]

    def dot(a, b):
        return jnp.dot(a, b, preferred_element_type=F32)

    def pick(tab, pos_ref, lo, n, stride, base, gath_lo, first, m=512):
        table = tab[...].reshape(-1, width)
        block = tab.shape[1]

        @pl.loop(0, n // m)
        def _(i):
            p = pos_ref[pl.ds(pl.multiple_of(lo + i * m, m), m), :]
            lane = lax.broadcasted_iota(jnp.int16, (m, 128), 1)
            q = p - lane
            parts = []
            for o in range(WIN):
                for h in range(block // 128):
                    parts.append(jnp.where(q == jnp.int16(o * stride + base + h * 128), BF(1), BF(0)))
            hot = jnp.concatenate(parts, axis=1)
            got = dot(hot, table)
            at = pl.ds(pl.multiple_of(gath_lo + i * m, m), m)
            if first:
                gath[at, :] = got.astype(BF)
            else:
                gath[at, :] = (gath[at, :].astype(F32) + got).astype(BF)

    def message(recv_ref, recv_lo, wt_ref, lo, slots, out_ref, tile=32):
        @pl.loop(0, m_rows // tile)
        def _(i):
            half = recv_ref[pl.ds(pl.multiple_of(recv_lo + i * tile, tile), tile), :].astype(F32) * 0.5
            acc = jnp.zeros((tile, width), F32)
            for s in range(slots):
                g = gath[pl.ds(pl.multiple_of(s * m_rows + i * tile, tile), tile), :].astype(F32)
                h = g + half
                w = wt_ref[pl.ds(pl.multiple_of(lo + s * m_rows + i * tile, tile), tile), :]
                acc = acc + jnp.concatenate([w] * (width // 128), axis=1) * (h + h * jnp.tanh(h))
            out_ref[pl.ds(pl.multiple_of(i * tile, tile), tile), :] = acc.astype(BF)

    def etab_q(q):
        return (
            lambda o: etab.at[q, o + SPAN],
            lambda d: et_s.at[q, d + SPAN],
            lambda o: et_r.at[q, o + SPAN],
        )

    for q in range(CH):
        g = grid_g[q]
        g.forward()
        acc = dot(grid_state[pl.ds(q * cr, cr), :], wrows(enc_send, 0))
        g.to_core.wait_recv()
        acc = acc + dot(gbuf[0, q], wrows(enc_send, 1)) + dot(gbuf[1, q], wrows(enc_send, 2))
        g.onward.wait_recv()
        acc = acc + dot(gbuf[2, q], wrows(enc_send, 3))
        etab[q, SPAN] = (acc * 0.5).astype(BF)
        exchange_start(*etab_q(q))

    ms_g.forward()
    eo_g = whole(enc_out, eobuf, eo_s, eo_r)
    eo_g.start()
    po_g = whole(proc_out, pobuf, po_s, po_r)
    e_rows = epos.shape[0]
    for q in range(CH):
        exchange_recv(*etab_q(q))
        pick(etab.at[q], epos, 0, e_rows, g_rows, q * cr, 0, q == 0)
        if q == 1:
            eo_g.forward()
            po_g.start()
    message(mesh_state, 0, ewt, 0, ei_ref.shape[0], agg1.at[0])
    a_g = Gather(agg1.at[0], lambda s: agg1.at[s + 1], lambda s: a1_s.at[s], lambda s: a1_r.at[s])
    a_g.start()
    ms_g.finish()
    eo_g.finish()
    po_g.forward()
    a_g.forward()
    a_g.finish()

    def update(state, agg, w_own, w_buf, out):
        for j in range(4):
            w_ref = w_own if j == 0 else w_buf.at[j - 1]
            acc = state(j).astype(F32)
            for i in range(4):
                acc = acc + dot(agg[i], wrows(w_ref, i))
            out[j] = acc.astype(BF)

    def project(m, w_ref, tab):
        acc = dot(m[0], wrows(w_ref, 0))
        for j in range(1, 4):
            acc = acc + dot(m[j], wrows(w_ref, j))
        tab[SPAN] = (acc * 0.5).astype(BF)

    update(lambda j: mesh_state[...] if j == 0 else msbuf[j - 1], agg1, enc_out, eobuf, m1)

    project(m1, proc_send, ptab)
    pt = (lambda o: ptab.at[o + SPAN], lambda d: pt_s.at[d + SPAN], lambda o: pt_r.at[o + SPAN])
    exchange_start(*pt)
    exchange_recv(*pt)
    pick(ptab, ppos, 0, ppos.shape[0], m_rows, 0, 0, True)
    message(m1.at[0], 0, pwt, 0, pi_ref.shape[0], agg2.at[0])
    b_g = Gather(agg2.at[0], lambda s: agg2.at[s + 1], lambda s: a2_s.at[s], lambda s: a2_r.at[s])
    b_g.start()
    po_g.finish()
    b_g.forward()
    b_g.finish()
    update(lambda j: m1[j], agg2, proc_out, pobuf, mn)

    project(mn, dec_send, dtab)
    dt = (lambda o: dtab.at[o + SPAN], lambda d: dt_s.at[d + SPAN], lambda o: dt_r.at[o + SPAN])
    exchange_start(*dt)
    mesh_next[...] = mn[0]
    exchange_recv(*dt)
    tiles = g_rows // m_rows
    d_slots = di_ref.shape[0]
    per = d_slots * m_rows
    out_g = []

    def write(t):
        at = pl.ds(t * m_rows, m_rows)
        acc = grid_state[at, :].astype(F32) + dot(agg3[0, t], wrows(dec_out, 0))
        out_g[t].finish()
        for j in range(1, 4):
            acc = acc + dot(agg3[j, t], wrows(dec_out, j))
        grid_next[at, :] = acc.astype(BF)

    for t in range(tiles):
        pick(dtab, dpos, t * per, per, m_rows, 0, 0, True)
        message(grid_state, t * m_rows, dwt, t * per, d_slots, agg3.at[0, t])
        g = Gather(
            agg3.at[0, t],
            lambda s, t=t: agg3.at[s + 1, t],
            lambda s, t=t: a3_s.at[s, t],
            lambda s, t=t: a3_r.at[s, t],
        )
        g.start()
        out_g.append(g)
        if t > 0:
            out_g[t - 1].forward()
    for t in range(tiles):
        if t == tiles - 1:
            out_g[t].forward()
        write(t)

    for g in pending:
        g.drain()
    for q in range(CH):
        exchange_drain(*etab_q(q))
    exchange_drain(*pt)
    exchange_drain(*dt)


def shards(*args):
    grid_state, mesh_state = args[:2]
    n_region = lax.axis_size("region")
    assert lax.axis_size("chan") == 4
    g_rows, width = grid_state.shape
    m_rows = mesh_state.shape[0]
    full = args[2].shape[0]
    cr = g_rows // CH
    tiles = g_rows // m_rows
    ke, kp, kd = args[8].shape[0], args[11].shape[0], args[14].shape[0]
    args = list(args)
    for i in (10, 13, 16):
        args[i] = args[i].reshape(1, -1)
    dma = pltpu.SemaphoreType.DMA
    V = pltpu.VMEM
    lanes = 128
    scratch = [
        V((3, CH, cr, width), BF),
        V((3, m_rows, width), BF),
        V((3, full, width), BF),
        V((3, full, width), BF),
        V((CH, WIN, cr, width), BF),
        V((WIN, m_rows, width), BF),
        V((WIN, m_rows, width), BF),
        V((ke * m_rows, lanes), jnp.int16),
        V((ke * m_rows, lanes), F32),
        V((kp * m_rows, lanes), jnp.int16),
        V((kp * m_rows, lanes), F32),
        V((kd * g_rows, lanes), jnp.int16),
        V((kd * g_rows, lanes), F32),
        V((ke * m_rows, width), BF),
        V((4, m_rows, width), BF),
        V((4, m_rows, width), BF),
        V((4, tiles, m_rows, width), BF),
        V((4, m_rows, width), BF),
        V((4, m_rows, width), BF),
        dma((3, CH)),
        dma((3, CH)),
        dma((3,)),
        dma((3,)),
        dma((3,)),
        dma((3,)),
        dma((3,)),
        dma((3,)),
        dma((3,)),
        dma((3,)),
        dma((3,)),
        dma((3,)),
        dma((3, tiles)),
        dma((3, tiles)),
        dma((CH, WIN)),
        dma((CH, WIN)),
        dma((WIN,)),
        dma((WIN,)),
        dma((WIN,)),
        dma((WIN,)),
    ]
    return pl.pallas_call(
        functools.partial(kernel, n_region),
        out_shape=(
            jax.ShapeDtypeStruct((g_rows, width), BF),
            jax.ShapeDtypeStruct((m_rows, width), BF),
        ),
        in_specs=[pl.BlockSpec(memory_space=pltpu.VMEM)] * 17,
        out_specs=(pl.BlockSpec(memory_space=pltpu.VMEM),) * 2,
        scratch_shapes=scratch,
        compiler_params=pltpu.CompilerParams(
            collective_id=0, has_side_effects=True, vmem_limit_bytes=56 * 1024 * 1024
        ),
    )(*args)


def solution(mesh):
    placed = (
        P("region", "chan"),
        P("region", "chan"),
        P(None, "chan"),
        P(None, "chan"),
        P(None, "chan"),
        P(None, "chan"),
        P(None, "chan"),
        P(None, "chan"),
        P(None, "region"),
        P(None, "region"),
        P("region"),
        P(None, "region"),
        P(None, "region"),
        P("region"),
        P(None, "region"),
        P(None, "region"),
        P("region"),
    )
    return jax.shard_map(
        shards,
        mesh=mesh,
        in_specs=placed,
        out_specs=(P("region", "chan"), P("region", "chan")),
        check_vma=False,
    )
```

time: 220 us -> 97.6 us (0.44)
  Pallas kernels: 0 us -> 94.2 us
  waiting for transfers between devices: 85.8 us -> 0 us
  local copies, waits for them, and re-layouts: 40.8 us -> 2.56 us
  blocking collectives: 30.6 us -> 0 us
  starting transfers between devices: 22.3 us -> 0 us
  other arithmetic: 18.3 us -> 0 us
  between operations: 14.6 us -> 0.65 us
  matrix products: 6.67 us -> 0 us
    pallas_call x0 -> x1, Pallas kernels: none -> 94.2 us  [shards(): pl.pallas_call(functools.partial(kernel, n_region), out_shape=(jax.ShapeD...]
    all_gather x2 -> x0, waiting for transfers between devices: 45.8 us -> none  [project(): lax.all_gather(values, 'chan', axis=1, tiled=True)]
    gather x3 -> x0, local copies, waits for them, and re-layouts: 40.4 us -> none  [messages(): fetched = jnp.take(projected, index_block, axis=0).astype(jnp.float32)]
    ppermute x12 -> x0, waiting for transfers between devices: 39.3 us -> none  [from_behind(): return lax.ppermute(shard, axis, pairs)]
    all_gather x4 -> x0, blocking collectives: 30.6 us -> none  [project(): lax.all_gather(values, 'chan', axis=1, tiled=True)]
    ppermute x12 -> x0, starting transfers between devices: 22.3 us -> none  [from_behind(): return lax.ppermute(shard, axis, pairs)]
    reduce_sum x3 -> x0, other arithmetic: 12.1 us -> none  [messages(): summed = jnp.sum(jnp.where(valid[:, :, None], message, 0.0), axis=0)]
    dot_general x6 -> x0, matrix products: 6.67 us -> none  [project(): jnp.dot(lax.all_gather(values, 'chan', axis=1, tiled=True), weight, prefe...]
  transfers between devices with their start and end apart: 14 -> 0, of which waited for: 9 -> 0; matrix products, arithmetic and copies ran while one was open for 2% -> 0% of each run, Pallas kernels for 0% -> 0%
where the time goes in v1:
time: 97.6 us; the launch traced here: 97.4 us
  Pallas kernels  94.2 us (97%)
  local copies, waits for them, and re-layouts  2.56 us (3%)
    pallas_call x1, Pallas kernels, shards(): pl.pallas_call(functools.partial(kernel, n_region), out_shape=(jax.ShapeD...  94.2 us
    unnamed x4, local copies, waits for them, and re-layouts  2.56 us

profile of v1, /device:TPU:1, one launch (start us, length us, event | category | flops | bytes accessed | tf_op | source)
XLA Modules:
  0.0 97.4 jit_solution(3251597684512562185)
XLA Ops:
  0.6 94.2 %shard_map.176 = (bf16[1024,256]{1,0:T(8,128)(2,1)}, bf16[256,256]{1,0:T(8,128)(2,1)}) custom-call(bf16[1024,256]{1,0:T(8,128)(2,1)} %grid_state.1, bf16[256,256]{1,0:T(8,128)(2,1)} %mesh_state.1, bf16[1024,256]{1,0:T(8,128)(2,1)} %enc_send.1, bf16[1024,256]{1,0:T(8,128)(2,1)} %enc_out.1, bf16[1024,256]{1,0:T(8,128)(2,1)} %proc_send.1, ...), custom_call_target="tpu_custom_call" | custom-call | tf_op jit(solution)/shard_map/pallas_call | solution.py:416
  94.8 0.0 copy-start
  94.8 1.9 %copy.21 = bf16[1024,256]{1,0:T(8,128)(2,1)} copy(bf16[1024,256]{1,0:T(8,128)(2,1)} %get-tuple-element.4) | data formatting | bytes 1048576
  96.8 0.0 copy-done
  96.8 0.7 copy.22
Async XLA Ops:
  94.8 1.9 %copy-start = (bf16[256,256]{1,0:T(8,128)(2,1)S(1)}, bf16[256,256]{1,0:T(8,128)(2,1)}, u32[]{:S(2)}) copy-start(bf16[256,256]{1,0:T(8,128)(2,1)} %get-tuple-element.5) | copy-start | bytes 393220

commit v2 on v1

--- a/solution.py
+++ b/solution.py
@@ -40,6 +40,13 @@
     msbuf,
     eobuf,
     pobuf,
+    wms,
+    wi,
+    ww,
+    wc,
+    part,
+    precv,
+    own32,
     etab,
     ptab,
     dtab,
@@ -50,6 +57,7 @@
     dpos,
     dwt,
     gath,
+    got,
     agg1,
     agg2,
     agg3,
@@ -69,8 +77,10 @@
     a2_r,
     a3_s,
     a3_r,
-    et_s,
-    et_r,
+    wn_s,
+    wn_r,
+    pp_s,
+    pp_r,
     pt_s,
     pt_r,
     dt_s,
@@ -157,6 +167,16 @@
             def _(d=d):
                 exchange(tab, ssem, rsem, d).wait_send()
 
+    window = []
+    for at, (own, buf) in enumerate(((ei_ref, wi), (ew_ref, ww), (ec_ref, wc), (mesh_state, wms))):
+        window.append((
+            lambda o, own=own, buf=buf: own if o == 0 else buf.at[o + SPAN],
+            lambda d, at=at: wn_s.at[at, d + SPAN],
+            lambda o, at=at: wn_r.at[at, o + SPAN],
+        ))
+    for w in window[:3]:
+        exchange_start(*w)
+
     grid_g = []
     for q in range(CH):
         rows = pl.ds(q * cr, cr)
@@ -174,37 +194,34 @@
 
     ms_g = whole(mesh_state, msbuf, ms_s, ms_r)
     ms_g.start()
+    exchange_start(*window[3])
 
     for o in OFFSETS:
         @pl.when(jnp.logical_not(inside(o)))
         def _(o=o):
-            for q in range(CH):
-                etab[q, o + SPAN] = jnp.zeros((cr, width), BF)
+            precv[o + SPAN] = jnp.zeros((m_rows, width), BF)
             ptab[o + SPAN] = jnp.zeros((m_rows, width), BF)
             dtab[o + SPAN] = jnp.zeros((m_rows, width), BF)
 
-    def edges(idx_ref, w_ref, cnt_ref, rows_per_region, pos_ref, wt_ref):
-        slots, recv = idx_ref.shape
-        first = (r - SPAN) * rows_per_region
-        tile = m_rows
-        for t in range(recv // tile):
-            cols = pl.ds(t * tile, tile)
-            cnt = cnt_ref[:, cols]
-            k = lax.broadcasted_iota(jnp.int32, (slots, tile), 0)
-            w = jnp.where(k < cnt, w_ref[:, cols], 0.0) / cnt.astype(F32)
-            p = (idx_ref[:, cols] - first).astype(F32)
-            pad = jnp.zeros((128 - 2 * slots, tile), F32)
-            both = jnp.concatenate([w, p, pad], axis=0).T
-            for s in range(slots):
-                at = pl.ds((t * slots + s) * tile, tile)
-                wt_ref[at, :] = jnp.broadcast_to(both[:, s : s + 1], (tile, 128))
-                pos_ref[at, :] = jnp.broadcast_to(
-                    both[:, slots + s : slots + s + 1].astype(jnp.int32), (tile, 128)
-                ).astype(jnp.int16)
-
-    edges(ei_ref, ew_ref, ec_ref, g_rows, epos, ewt)
-    edges(pi_ref, pw_ref, pc_ref, m_rows, ppos, pwt)
-    edges(di_ref, dw_ref, dc_ref, m_rows, dpos, dwt)
+    def edges(idx, w_all, cnt_all, first, length, tile, pos_ref, wt_ref):
+        slots, recv = idx.shape
+        for t in range(recv // m_rows):
+            cols = slice(t * m_rows, (t + 1) * m_rows)
+            cnt = cnt_all[:, cols]
+            p = idx[:, cols] - first
+            k = lax.broadcasted_iota(jnp.int32, (slots, m_rows), 0)
+            live = (k < cnt) & (p >= 0) & (p < length)
+            w = jnp.where(live, w_all[:, cols], 0.0) / cnt.astype(F32)
+            pad = jnp.zeros((128 - 2 * slots, m_rows), F32)
+            both = jnp.concatenate([w, p.astype(F32), pad], axis=0).T
+            for u in range(m_rows // tile):
+                mine = both[u * tile : (u + 1) * tile, :]
+                for s in range(slots):
+                    at = pl.ds(((t * (m_rows // tile) + u) * slots + s) * tile, tile)
+                    wt_ref[at, :] = jnp.broadcast_to(mine[:, s : s + 1], (tile, 128))
+                    pos_ref[at, :] = jnp.broadcast_to(
+                        mine[:, slots + s : slots + s + 1].astype(jnp.int32), (tile, 128)
+                    ).astype(jnp.int16)
 
     def wrows(w_ref, j):
         return w_ref[pl.ds(pl.multiple_of(rel[j] * width, width), width), :]
@@ -212,76 +229,141 @@
     def dot(a, b):
         return jnp.dot(a, b, preferred_element_type=F32)
 
-    def pick(tab, pos_ref, lo, n, stride, base, gath_lo, first, m=512):
-        table = tab[...].reshape(-1, width)
-        block = tab.shape[1]
-
-        @pl.loop(0, n // m)
+    def hot(pos_ref, at, m, base, length):
+        q = pos_ref[at, :] - lax.broadcasted_iota(jnp.int16, (m, 128), 1)
+        parts = [
+            jnp.where(q == jnp.int16(base + lane), BF(1), BF(0)) for lane in range(0, length, 128)
+        ]
+        return jnp.concatenate(parts, axis=1)
+
+    def messages(table, base, pos_ref, wt_ref, lo, slots, tile, tiles, recv_ref, recv_lo, out_ref, prior=None, sub=32):
+        m = slots * tile
+
+        @pl.loop(0, tiles)
         def _(i):
-            p = pos_ref[pl.ds(pl.multiple_of(lo + i * m, m), m), :]
-            lane = lax.broadcasted_iota(jnp.int16, (m, 128), 1)
-            q = p - lane
-            parts = []
-            for o in range(WIN):
-                for h in range(block // 128):
-                    parts.append(jnp.where(q == jnp.int16(o * stride + base + h * 128), BF(1), BF(0)))
-            hot = jnp.concatenate(parts, axis=1)
-            got = dot(hot, table)
-            at = pl.ds(pl.multiple_of(gath_lo + i * m, m), m)
-            if first:
-                gath[at, :] = got.astype(BF)
+            at = pl.ds(pl.multiple_of(lo + i * m, m), m)
+            new = dot(hot(pos_ref, at, m, base, table.shape[0]), table)
+            if prior is not None:
+                new = new + prior[pl.ds(pl.multiple_of(i * m, m), m), :].astype(F32)
+            got[...] = new
+
+            @pl.loop(0, tile // sub)
+            def _(j):
+                off = pl.multiple_of(j * sub, sub)
+                rows = pl.ds(pl.multiple_of(recv_lo + i * tile + off, sub), sub)
+                half = recv_ref[rows, :].astype(F32) * 0.5
+                acc = jnp.zeros((sub, width), F32)
+                for s in range(slots):
+                    h = got[pl.ds(pl.multiple_of(s * tile + off, sub), sub), :] + half
+                    w = wt_ref[pl.ds(pl.multiple_of(lo + i * m + s * tile + off, sub), sub), :]
+                    acc = acc + jnp.concatenate([w] * (width // 128), axis=1) * (h + h * jnp.tanh(h))
+                out_ref[pl.ds(pl.multiple_of(i * tile + off, sub), sub), :] = acc.astype(out_ref.dtype)
+
+    ke, kp, kd = ei_ref.shape[0], pi_ref.shape[0], di_ref.shape[0]
+    e_tile, p_tile, d_tile = got.shape[0] // ke, got.shape[0] // kp, got.shape[0] // kd
+    e_rows = ke * m_rows
+    order = (2, -2, 1, -1, 0)
+
+    def here(o, body):
+        if o == 0:
+            body()
+        else:
+            pl.when(inside(o))(body)
+
+    def window_edges(o):
+        def body():
+            if o == 0:
+                data = ei_ref[...], ew_ref[...], ec_ref[...]
             else:
-                gath[at, :] = (gath[at, :].astype(F32) + got).astype(BF)
-
-    def message(recv_ref, recv_lo, wt_ref, lo, slots, out_ref, tile=32):
-        @pl.loop(0, m_rows // tile)
-        def _(i):
-            half = recv_ref[pl.ds(pl.multiple_of(recv_lo + i * tile, tile), tile), :].astype(F32) * 0.5
-            acc = jnp.zeros((tile, width), F32)
-            for s in range(slots):
-                g = gath[pl.ds(pl.multiple_of(s * m_rows + i * tile, tile), tile), :].astype(F32)
-                h = g + half
-                w = wt_ref[pl.ds(pl.multiple_of(lo + s * m_rows + i * tile, tile), tile), :]
-                acc = acc + jnp.concatenate([w] * (width // 128), axis=1) * (h + h * jnp.tanh(h))
-            out_ref[pl.ds(pl.multiple_of(i * tile, tile), tile), :] = acc.astype(BF)
-
-    def etab_q(q):
-        return (
-            lambda o: etab.at[q, o + SPAN],
-            lambda d: et_s.at[q, d + SPAN],
-            lambda o: et_r.at[q, o + SPAN],
-        )
-
-    for q in range(CH):
+                for w in window[:3]:
+                    exchange(*w, -o).wait_recv()
+                data = wi[o + SPAN], ww[o + SPAN], wc[o + SPAN]
+            edges(*data, r * g_rows, g_rows, e_tile, epos.at[o + SPAN], ewt.at[o + SPAN])
+
+        here(o, body)
+
+    def project_grid(q):
         g = grid_g[q]
-        g.forward()
         acc = dot(grid_state[pl.ds(q * cr, cr), :], wrows(enc_send, 0))
         g.to_core.wait_recv()
         acc = acc + dot(gbuf[0, q], wrows(enc_send, 1)) + dot(gbuf[1, q], wrows(enc_send, 2))
         g.onward.wait_recv()
         acc = acc + dot(gbuf[2, q], wrows(enc_send, 3))
-        etab[q, SPAN] = (acc * 0.5).astype(BF)
-        exchange_start(*etab_q(q))
-
-    ms_g.forward()
+        etab[pl.ds(q * cr, cr), :] = (acc * 0.5).astype(BF)
+
+    early = g_rows // 2
+
+    def first_half(o):
+        def body():
+            m = 2048
+
+            @pl.loop(0, e_rows // m)
+            def _(i):
+                at = pl.ds(pl.multiple_of(i * m, m), m)
+                gath[o + SPAN, at, :] = dot(
+                    hot(epos.at[o + SPAN], at, m, 0, early), etab[pl.ds(0, early), :]
+                ).astype(BF)
+
+        here(o, body)
+
+    def back(d):
+        return rcopy(part.at[d + SPAN], precv.at[SPAN - d], pp_s.at[d + SPAN], pp_r.at[SPAN - d],
+                     ((r + d + n_region) % n_region, c))
+
+    def second_half(o):
+        def body():
+            if o != 0:
+                exchange(*window[3], -o).wait_recv()
+            messages(
+                etab[pl.ds(early, g_rows - early), :], early, epos.at[o + SPAN], ewt.at[o + SPAN], 0,
+                ke, e_tile, m_rows // e_tile, mesh_state if o == 0 else wms.at[o + SPAN], 0,
+                own32 if o == 0 else part.at[o + SPAN], gath.at[o + SPAN],
+            )
+            if o != 0:
+                back(o).start()
+
+        here(o, body)
+
+    window_edges(0)
+    grid_g[0].forward()
+    window_edges(1)
+    project_grid(0)
+    grid_g[1].forward()
+    window_edges(-1)
+    project_grid(1)
+    grid_g[2].forward()
+    window_edges(2)
+    window_edges(-2)
+    for o in order:
+        first_half(o)
+        if o == -2:
+            grid_g[3].forward()
+            ms_g.forward()
     eo_g = whole(enc_out, eobuf, eo_s, eo_r)
     eo_g.start()
+    project_grid(2)
+    project_grid(3)
+    for o in order:
+        second_half(o)
+        if o == 1:
+            eo_g.forward()
     po_g = whole(proc_out, pobuf, po_s, po_r)
-    e_rows = epos.shape[0]
-    for q in range(CH):
-        exchange_recv(*etab_q(q))
-        pick(etab.at[q], epos, 0, e_rows, g_rows, q * cr, 0, q == 0)
-        if q == 1:
-            eo_g.forward()
-            po_g.start()
-    message(mesh_state, 0, ewt, 0, ei_ref.shape[0], agg1.at[0])
+    total = own32[...]
+    for o in OFFSETS:
+        @pl.when(inside(o))
+        def _(o=o):
+            back(-o).wait_recv()
+    for o in OFFSETS:
+        total = total + precv[o + SPAN].astype(F32)
+    agg1[0] = total.astype(BF)
     a_g = Gather(agg1.at[0], lambda s: agg1.at[s + 1], lambda s: a1_s.at[s], lambda s: a1_r.at[s])
     a_g.start()
+    edges(pi_ref[...], pw_ref[...], pc_ref[...], (r - SPAN) * m_rows, WIN * m_rows, p_tile, ppos, pwt)
     ms_g.finish()
     eo_g.finish()
-    po_g.forward()
     a_g.forward()
     a_g.finish()
+    po_g.start()
 
     def update(state, agg, w_own, w_buf, out):
         for j in range(4):
@@ -302,9 +384,12 @@
     project(m1, proc_send, ptab)
     pt = (lambda o: ptab.at[o + SPAN], lambda d: pt_s.at[d + SPAN], lambda o: pt_r.at[o + SPAN])
     exchange_start(*pt)
+    edges(di_ref[...], dw_ref[...], dc_ref[...], (r - SPAN) * m_rows, WIN * m_rows, d_tile, dpos, dwt)
     exchange_recv(*pt)
-    pick(ptab, ppos, 0, ppos.shape[0], m_rows, 0, 0, True)
-    message(m1.at[0], 0, pwt, 0, pi_ref.shape[0], agg2.at[0])
+    messages(
+        ptab[...].reshape(-1, width), 0, ppos, pwt, 0, kp, p_tile, m_rows // p_tile, m1.at[0], 0, agg2.at[0]
+    )
+    po_g.forward()
     b_g = Gather(agg2.at[0], lambda s: agg2.at[s + 1], lambda s: a2_s.at[s], lambda s: a2_r.at[s])
     b_g.start()
     po_g.finish()
@@ -318,8 +403,7 @@
     mesh_next[...] = mn[0]
     exchange_recv(*dt)
     tiles = g_rows // m_rows
-    d_slots = di_ref.shape[0]
-    per = d_slots * m_rows
+    per = kd * m_rows
     out_g = []
 
     def write(t):
@@ -331,8 +415,10 @@
         grid_next[at, :] = acc.astype(BF)
 
     for t in range(tiles):
-        pick(dtab, dpos, t * per, per, m_rows, 0, 0, True)
-        message(grid_state, t * m_rows, dwt, t * per, d_slots, agg3.at[0, t])
+        messages(
+            dtab[...].reshape(-1, width), 0, dpos, dwt, t * per, kd, d_tile, m_rows // d_tile,
+            grid_state, t * m_rows, agg3.at[0, t],
+        )
         g = Gather(
             agg3.at[0, t],
             lambda s, t=t: agg3.at[s + 1, t],
@@ -350,8 +436,12 @@
 
     for g in pending:
         g.drain()
-    for q in range(CH):
-        exchange_drain(*etab_q(q))
+    for w in window:
+        exchange_drain(*w)
+    for d in OFFSETS:
+        @pl.when(inside(d))
+        def _(d=d):
+            back(d).wait_send()
     exchange_drain(*pt)
     exchange_drain(*dt)
 
@@ -377,16 +467,24 @@
         V((3, m_rows, width), BF),
         V((3, full, width), BF),
         V((3, full, width), BF),
-        V((CH, WIN, cr, width), BF),
+        V((WIN, m_rows, width), BF),
+        V((WIN, ke, m_rows), jnp.int32),
+        V((WIN, ke, m_rows), F32),
+        V((WIN, 1, m_rows), jnp.int32),
         V((WIN, m_rows, width), BF),
         V((WIN, m_rows, width), BF),
-        V((ke * m_rows, lanes), jnp.int16),
-        V((ke * m_rows, lanes), F32),
+        V((m_rows, width), F32),
+        V((g_rows, width), BF),
+        V((WIN, m_rows, width), BF),
+        V((WIN, m_rows, width), BF),
+        V((WIN, ke * m_rows, lanes), jnp.int16),
+        V((WIN, ke * m_rows, lanes), F32),
         V((kp * m_rows, lanes), jnp.int16),
         V((kp * m_rows, lanes), F32),
         V((kd * g_rows, lanes), jnp.int16),
         V((kd * g_rows, lanes), F32),
-        V((ke * m_rows, width), BF),
+        V((WIN, ke * m_rows, width), BF),
+        V((1024, width), F32),
         V((4, m_rows, width), BF),
         V((4, m_rows, width), BF),
         V((4, tiles, m_rows, width), BF),
@@ -406,8 +504,10 @@
         dma((3,)),
         dma((3, tiles)),
         dma((3, tiles)),
-        dma((CH, WIN)),
-        dma((CH, WIN)),
+        dma((4, WIN)),
+        dma((4, WIN)),
+        dma((WIN,)),
+        dma((WIN,)),
         dma((WIN,)),
         dma((WIN,)),
         dma((WIN,)),

time: 97.6 us -> 101 us (1.035)
  Pallas kernels: 94.2 us -> 97.8 us
    pallas_call x1, Pallas kernels: 94.2 us -> 97.8 us  [shards(): pl.pallas_call(functools.partial(kernel, n_region), out_shape=(jax.ShapeD...]
where the time goes in v2:
time: 101 us
  Pallas kernels  97.8 us (97%)
  local copies, waits for them, and re-layouts  2.56 us (3%)
    pallas_call x1, Pallas kernels, shards(): pl.pallas_call(functools.partial(kernel, n_region), out_shape=(jax.ShapeD...  97.8 us
    unnamed x4, local copies, waits for them, and re-layouts  2.56 us

profile of v2, /device:TPU:1, one launch (start us, length us, event | category | flops | bytes accessed | tf_op | source)
XLA Modules:
  0.0 101.0 jit_solution(3639241903621968311)
XLA Ops:
  0.6 97.8 %shard_map.176 = (bf16[1024,256]{1,0:T(8,128)(2,1)}, bf16[256,256]{1,0:T(8,128)(2,1)}) custom-call(bf16[1024,256]{1,0:T(8,128)(2,1)} %grid_state.1, bf16[256,256]{1,0:T(8,128)(2,1)} %mesh_state.1, bf16[1024,256]{1,0:T(8,128)(2,1)} %enc_send.1, bf16[1024,256]{1,0:T(8,128)(2,1)} %enc_out.1, bf16[1024,256]{1,0:T(8,128)(2,1)} %proc_send.1, ...), custom_call_target="tpu_custom_call" | custom-call | tf_op jit(solution)/shard_map/pallas_call | solution.py:516
  98.5 0.0 copy-start
  98.5 1.9 %copy.21 = bf16[1024,256]{1,0:T(8,128)(2,1)} copy(bf16[1024,256]{1,0:T(8,128)(2,1)} %get-tuple-element.4) | data formatting | bytes 1048576
  100.4 0.0 copy-done
  100.4 0.7 copy.22
Async XLA Ops:
  98.5 1.9 %copy-start = (bf16[256,256]{1,0:T(8,128)(2,1)S(1)}, bf16[256,256]{1,0:T(8,128)(2,1)}, u32[]{:S(2)}) copy-start(bf16[256,256]{1,0:T(8,128)(2,1)} %get-tuple-element.5) | copy-start | bytes 393220

commit v3 on v2

--- a/solution.py
+++ b/solution.py
@@ -20,11 +20,11 @@
     grid_state,
     mesh_state,
     enc_send,
-    enc_out,
-    proc_send,
-    proc_out,
-    dec_send,
-    dec_out,
+    enc_out_hbm,
+    proc_send_hbm,
+    proc_out_hbm,
+    dec_send_hbm,
+    dec_out_hbm,
     ei_ref,
     ew_ref,
     ec_ref,
@@ -36,6 +36,12 @@
     dc_ref,
     grid_next,
     mesh_next,
+    enc_out,
+    proc_send,
+    proc_out,
+    dec_send,
+    dec_out,
+    load_sem,
     gbuf,
     msbuf,
     eobuf,
@@ -177,6 +183,14 @@
     for w in window[:3]:
         exchange_start(*w)
 
+    loads = [
+        pltpu.make_async_copy(a, b, load_sem.at[i])
+        for i, (a, b) in enumerate((
+            (enc_out_hbm, enc_out), (proc_out_hbm, proc_out), (proc_send_hbm, proc_send),
+            (dec_send_hbm, dec_send), (dec_out_hbm, dec_out),
+        ))
+    ]
+
     grid_g = []
     for q in range(CH):
         rows = pl.ds(q * cr, cr)
@@ -195,6 +209,8 @@
     ms_g = whole(mesh_state, msbuf, ms_s, ms_r)
     ms_g.start()
     exchange_start(*window[3])
+    for load in loads:
+        load.start()
 
     for o in OFFSETS:
         @pl.when(jnp.logical_not(inside(o)))
@@ -218,7 +234,7 @@
                 mine = both[u * tile : (u + 1) * tile, :]
                 for s in range(slots):
                     at = pl.ds(((t * (m_rows // tile) + u) * slots + s) * tile, tile)
-                    wt_ref[at, :] = jnp.broadcast_to(mine[:, s : s + 1], (tile, 128))
+                    wt_ref[at, :] = jnp.broadcast_to(mine[:, s : s + 1], (tile, 128)).astype(BF)
                     pos_ref[at, :] = jnp.broadcast_to(
                         mine[:, slots + s : slots + s + 1].astype(jnp.int32), (tile, 128)
                     ).astype(jnp.int16)
@@ -242,25 +258,26 @@
         @pl.loop(0, tiles)
         def _(i):
             at = pl.ds(pl.multiple_of(lo + i * m, m), m)
-            new = dot(hot(pos_ref, at, m, base, table.shape[0]), table)
-            if prior is not None:
-                new = new + prior[pl.ds(pl.multiple_of(i * m, m), m), :].astype(F32)
-            got[...] = new
-
-            @pl.loop(0, tile // sub)
-            def _(j):
-                off = pl.multiple_of(j * sub, sub)
+            got[pl.ds(0, m), :] = dot(hot(pos_ref, at, m, base, table.shape[0]), table).astype(BF)
+            for off in range(0, tile, sub):
                 rows = pl.ds(pl.multiple_of(recv_lo + i * tile + off, sub), sub)
-                half = recv_ref[rows, :].astype(F32) * 0.5
+                half = recv_ref[rows, :] * BF(0.5)
                 acc = jnp.zeros((sub, width), F32)
-                for s in range(slots):
-                    h = got[pl.ds(pl.multiple_of(s * tile + off, sub), sub), :] + half
-                    w = wt_ref[pl.ds(pl.multiple_of(lo + i * m + s * tile + off, sub), sub), :]
-                    acc = acc + jnp.concatenate([w] * (width // 128), axis=1) * (h + h * jnp.tanh(h))
+                for s in range(0, slots, 4):
+                    four = []
+                    for z in range(s, s + 4):
+                        h = got[pl.ds(z * tile + off, sub), :]
+                        if prior is not None:
+                            h = h + prior[pl.ds(pl.multiple_of(i * m + z * tile + off, sub), sub), :]
+                        h = h + half
+                        w = wt_ref[pl.ds(pl.multiple_of(lo + i * m + z * tile + off, sub), sub), :]
+                        w = jnp.concatenate([w] * (width // 128), axis=1)
+                        four.append(w * (h + h * jnp.tanh(h)))
+                    acc = acc + ((four[0] + four[1]) + (four[2] + four[3])).astype(F32)
                 out_ref[pl.ds(pl.multiple_of(i * tile + off, sub), sub), :] = acc.astype(out_ref.dtype)
 
     ke, kp, kd = ei_ref.shape[0], pi_ref.shape[0], di_ref.shape[0]
-    e_tile, p_tile, d_tile = got.shape[0] // ke, got.shape[0] // kp, got.shape[0] // kd
+    e_tile, p_tile, d_tile = 2048 // ke, 1024 // kp, 1024 // kd
     e_rows = ke * m_rows
     order = (2, -2, 1, -1, 0)
 
@@ -339,6 +356,8 @@
         if o == -2:
             grid_g[3].forward()
             ms_g.forward()
+    for load in loads:
+        load.wait()
     eo_g = whole(enc_out, eobuf, eo_s, eo_r)
     eo_g.start()
     project_grid(2)
@@ -386,15 +405,27 @@
     exchange_start(*pt)
     edges(di_ref[...], dw_ref[...], dc_ref[...], (r - SPAN) * m_rows, WIN * m_rows, d_tile, dpos, dwt)
     exchange_recv(*pt)
-    messages(
-        ptab[...].reshape(-1, width), 0, ppos, pwt, 0, kp, p_tile, m_rows // p_tile, m1.at[0], 0, agg2.at[0]
-    )
+    b_g = []
+    p_rows = kp * p_tile
+    for t in range(m_rows // p_tile):
+        at = pl.ds(t * p_tile, p_tile)
+        messages(
+            ptab[...].reshape(-1, width), 0, ppos, pwt, t * p_rows, kp, p_tile, 1, m1.at[0], t * p_tile, agg2.at[0, at]
+        )
+        g = Gather(
+            agg2.at[0, at],
+            lambda s, at=at: agg2.at[s + 1, at],
+            lambda s, t=t: a2_s.at[s, t],
+            lambda s, t=t: a2_r.at[s, t],
+        )
+        g.start()
+        b_g.append(g)
     po_g.forward()
-    b_g = Gather(agg2.at[0], lambda s: agg2.at[s + 1], lambda s: a2_s.at[s], lambda s: a2_r.at[s])
-    b_g.start()
+    for g in b_g:
+        g.forward()
     po_g.finish()
-    b_g.forward()
-    b_g.finish()
+    for g in b_g:
+        g.finish()
     update(lambda j: m1[j], agg2, proc_out, pobuf, mn)
 
     project(mn, dec_send, dtab)
@@ -463,6 +494,8 @@
     V = pltpu.VMEM
     lanes = 128
     scratch = [
+        *[V((full, width), BF) for _ in range(5)],
+        dma((5,)),
         V((3, CH, cr, width), BF),
         V((3, m_rows, width), BF),
         V((3, full, width), BF),
@@ -478,13 +511,13 @@
         V((WIN, m_rows, width), BF),
         V((WIN, m_rows, width), BF),
         V((WIN, ke * m_rows, lanes), jnp.int16),
-        V((WIN, ke * m_rows, lanes), F32),
+        V((WIN, ke * m_rows, lanes), BF),
         V((kp * m_rows, lanes), jnp.int16),
-        V((kp * m_rows, lanes), F32),
+        V((kp * m_rows, lanes), BF),
         V((kd * g_rows, lanes), jnp.int16),
-        V((kd * g_rows, lanes), F32),
+        V((kd * g_rows, lanes), BF),
         V((WIN, ke * m_rows, width), BF),
-        V((1024, width), F32),
+        V((2048, width), BF),
         V((4, m_rows, width), BF),
         V((4, m_rows, width), BF),
         V((4, tiles, m_rows, width), BF),
@@ -500,8 +533,8 @@
         dma((3,)),
         dma((3,)),
         dma((3,)),
-        dma((3,)),
-        dma((3,)),
+        dma((3, 2)),
+        dma((3, 2)),
         dma((3, tiles)),
         dma((3, tiles)),
         dma((4, WIN)),
@@ -519,7 +552,9 @@
             jax.ShapeDtypeStruct((g_rows, width), BF),
             jax.ShapeDtypeStruct((m_rows, width), BF),
         ),
-        in_specs=[pl.BlockSpec(memory_space=pltpu.VMEM)] * 17,
+        in_specs=[
+            pl.BlockSpec(memory_space=pl.ANY if 3 <= i <= 7 else pltpu.VMEM) for i in range(17)
+        ],
         out_specs=(pl.BlockSpec(memory_space=pltpu.VMEM),) * 2,
         scratch_shapes=scratch,
         compiler_params=pltpu.CompilerParams(

time: 101 us -> 96.7 us (0.957)
  Pallas kernels: 97.8 us -> 93.3 us
    pallas_call x1, Pallas kernels: 97.8 us -> 93.3 us  [shards(): pl.pallas_call(functools.partial(kernel, n_region), out_shape=(jax.ShapeD...]
where the time goes in v3:
time: 96.7 us; the launch traced here: 96.6 us
  Pallas kernels  93.3 us (96%)
  local copies, waits for them, and re-layouts  2.56 us (3%)
    pallas_call x1, Pallas kernels, shards(): pl.pallas_call(functools.partial(kernel, n_region), out_shape=(jax.ShapeD...  93.3 us
    unnamed x4, local copies, waits for them, and re-layouts  2.56 us

profile of v3, /device:TPU:1, one launch (start us, length us, event | category | flops | bytes accessed | tf_op | source)
XLA Modules:
  0.0 96.6 jit_solution(15477524415718065807)
XLA Ops:
  0.6 93.3 %shard_map.176 = (bf16[1024,256]{1,0:T(8,128)(2,1)}, bf16[256,256]{1,0:T(8,128)(2,1)}) custom-call(bf16[1024,256]{1,0:T(8,128)(2,1)} %grid_state.1, bf16[256,256]{1,0:T(8,128)(2,1)} %mesh_state.1, bf16[1024,256]{1,0:T(8,128)(2,1)} %enc_send.1, bf16[1024,256]{1,0:T(8,128)(2,1)} %enc_out_hbm.1, bf16[1024,256]{1,0:T(8,128)(2,1)} %proc_send_hbm.1, ...), custom_call_target="tpu_custom_call" | custom-call | tf_op jit(solution)/shard_map/pallas_call | solution.py:549
  94.0 0.0 copy-start
  94.0 1.9 %copy.21 = bf16[1024,256]{1,0:T(8,128)(2,1)} copy(bf16[1024,256]{1,0:T(8,128)(2,1)} %get-tuple-element.4) | data formatting | bytes 1048576
  95.9 0.0 copy-done
  95.9 0.7 copy.22
Async XLA Ops:
  94.0 1.9 %copy-start = (bf16[256,256]{1,0:T(8,128)(2,1)S(1)}, bf16[256,256]{1,0:T(8,128)(2,1)}, u32[]{:S(2)}) copy-start(bf16[256,256]{1,0:T(8,128)(2,1)} %get-tuple-element.5) | copy-start | bytes 393220
